TPU v7x, 512 devices: a whole 4x4x16 slice. The times are simulated.
512 devices in a mesh: row: 32 (over x, z_lo, core), col: 16 (over y, z_hi).
Axes of the slice: x: 4, y: 4, z: 16 (z_hi: 4, z_lo: 4; z = z_hi * 4 + z_lo), core: 2. Of those that a mesh axis runs over, the one named last changes fastest.
Arguments:
- site_tensor: bfloat16 [4096, 2, 4096], P('row', None, 'col'), may hold values from -6 to 6
- left_env: bfloat16 [16, 4096, 4096], P(None, 'row', 'col'), may hold values from -0.0234375 to 0.0234375
- right_env: bfloat16 [4096, 16, 768], P('row', None, 'col'), may hold values from -0.09375 to 0.09375
- mpo_out: int32 [48], replicated, may hold values from 0 to 15
- mpo_in: int32 [48], replicated, may hold values from 0 to 15
- mpo_ops: bfloat16 [48, 2, 2], replicated, may hold values from -3 to 3
Outputs:
- gradient: bfloat16 [4096, 2, 768], P('col', None, 'row')
All inputs are finite; a program needn't handle non-finite values.
Results may differ from a plain program's by a relative error of at most 0.0059.
Values may be sent and summed in bfloat16 or wider, within the bound.
A program may use at most 64 MiB of HBM per device.

v0:
```python
import jax
import jax.numpy as jnp
from jax import lax
from jax.sharding import PartitionSpec as P

MPOW = 16


def dense_mpo(mpo_out, mpo_in, mpo_ops):
    channels = jnp.arange(MPOW, dtype=jnp.int32)
    pick_out = (mpo_out[:, None] == channels[None, :]).astype(jnp.float32)
    pick_in = (mpo_in[:, None] == channels[None, :]).astype(jnp.float32)
    dense = jnp.einsum(
        "nw,nv,nst->wsvt",
        pick_out,
        pick_in,
        mpo_ops.astype(jnp.float32),
        precision=lax.Precision.HIGHEST,
    )
    return dense.astype(jnp.bfloat16)


def project(site_rows, env_panel):
    gathered = lax.all_gather(env_panel, "row", axis=0, tiled=True)
    product = jnp.dot(site_rows, gathered, preferred_element_type=jnp.float32)
    return product.astype(jnp.bfloat16)


def local(site_tensor, left_env, right_env, mpo_out, mpo_in, mpo_ops):
    row_block = site_tensor.shape[0]
    spin_states = site_tensor.shape[1]
    mpo_dense = dense_mpo(mpo_out, mpo_in, mpo_ops)
    whole_site = lax.all_gather(site_tensor, "col", axis=2, tiled=True)
    site_rows = whole_site.reshape(row_block * spin_states, whole_site.shape[2])
    mixed_rows = project(site_rows, right_env.reshape(right_env.shape[0], -1))
    by_columns = mixed_rows.reshape(row_block, spin_states, right_env.shape[1], right_env.shape[2])
    contracted = jnp.einsum(
        "wsvt,xtvb->wxsb", mpo_dense, by_columns, preferred_element_type=jnp.float32
    )
    channel = lax.all_gather(contracted.astype(jnp.bfloat16), "col", axis=3, tiled=True)
    bra_block = left_env.shape[2]
    flat_left = left_env.reshape(-1, bra_block)
    flat_channel = channel.reshape(flat_left.shape[0], -1)
    partial_grad = lax.dot_general(
        flat_left, flat_channel, (((0,), (0,)), ((), ())), preferred_element_type=jnp.float32
    )
    partial_grad = partial_grad.reshape(bra_block, spin_states, -1)
    return lax.psum_scatter(partial_grad, "row", scatter_dimension=2, tiled=True).astype(
        jnp.bfloat16
    )


def solution(mesh):
    return jax.shard_map(
        local,
        mesh=mesh,
        in_specs=(
            P("row", None, "col"),
            P(None, "row", "col"),
            P("row", None, "col"),
            P(),
            P(),
            P(),
        ),
        out_specs=P("col", None, "row"),
        check_vma=False,
    )
```

profile of v0, /device:TPU:1, one launch (start us, length us, event | category | flops | bytes accessed | tf_op | source)
XLA Modules:
  0.0 566.9 jit_solution(1353434308227548463)
XLA Ops:
  6.5 0.0 copy-start
  6.5 0.0 all-gather.4.cloned.1.call-start
  6.5 0.7 all-gather.4.cloned.1.call-update
  7.3 0.0 all-gather.6.cloned.1.call-start
  7.3 0.7 all-gather.6.cloned.1.call-update
  8.0 0.0 all-gather.8.cloned.1.call-start
  8.1 0.7 convert.7
  8.7 0.7 fusion.10
  9.4 0.8 fusion.5
  10.2 132.4 %all-gather.4.cloned.1.call-done = bf16[128,2,4096]{2,1,0:T(2,128)(2,1)} async-done(((bf16[128,2,256]{2,1,0:T(2,128)(2,1)}), bf16[128,2,4096]{2,1,0:T(2,128)(2,1)}) %all-gather.4.cloned.1.call-update) | async-done | bytes 2097168 | tf_op jit(solution)/shard_map/all_gather | solution.py:33
  142.6 2.7 reshape.20
  145.3 80.0 %all-gather.6.cloned.1.call-done = bf16[4096,768]{0,1:T(8,128)(2,1)} async-done(((bf16[128,768]{0,1:T(8,128)(2,1)}), bf16[4096,768]{0,1:T(8,128)(2,1)}) %all-gather.6.cloned.1.call-update) | async-done | bytes 6291472 | tf_op jit(solution)/shard_map/all_gather | solution.py:24
  225.3 4.6 convolution_convert_fusion
  230.0 1.2 reshape.22
  231.2 1.4 copy.15
  232.6 1.1 fusion.4
  233.7 0.0 all-gather.8.cloned.1.call-update
  233.7 0.0 reduce-scatter.2.cloned.1.call-start
  233.8 175.5 %all-gather.8.cloned.1.call-done = bf16[16,128,2,768]{1,0,2,3:T(8,128)(2,1)} async-done(((bf16[16,128,2,48]{1,0,2,3:T(8,128)(2,1)}), bf16[16,128,2,768]{1,0,2,3:T(8,128)(2,1)}) %all-gather.8.cloned.1.call-update) | async-done | bytes 6291472 | tf_op jit(solution)/shard_map/all_gather | solution.py:40
  409.3 3.9 copy.13
  413.1 0.0 copy-done
  413.1 3.0 fusion
  416.1 0.0 reduce-scatter.2.cloned.1.call-update
  416.1 142.9 %reduce-scatter.2.cloned.1.call-done = f32[256,2,24]{0,2,1:T(8,128)} async-done(((f32[256,2,768]{0,2,1:T(8,128)}), f32[256,2,24]{0,2,1:T(8,128)}) %reduce-scatter.2.cloned.1.call-update) | async-done | bytes 49168 | tf_op jit(solution)/shard_map/reduce_scatter | solution.py:48
  559.0 1.4 convert_element_type.26
Async XLA Ops:
  6.5 406.6 %copy-start = (bf16[16,128,256]{2,1,0:T(8,128)(2,1)S(1)}, bf16[16,128,256]{2,1,0:T(8,128)(2,1)}, u32[]{:S(2)}) copy-start(bf16[16,128,256]{2,1,0:T(8,128)(2,1)} %param.7) | copy-start | bytes 3145732
  6.5 136.1 %all-gather.4.cloned.1.call-start = ((), (), s32[]{:S(2)}) async-start(), calls=%async_computation.1 | async-start | bytes 2228224 | tf_op jit(solution)/shard_map/all_gather | solution.py:33
  7.3 218.1 %all-gather.6.cloned.1.call-start = ((), (), s32[]{:S(2)}) async-start(), calls=%async_computation.2 | async-start | bytes 6488064 | tf_op jit(solution)/shard_map/all_gather | solution.py:24
  8.0 401.2 %all-gather.8.cloned.1.call-start = ((), (), s32[]{:S(2)}) async-start(), calls=%async_computation.3 | async-start | bytes 6684672 | tf_op jit(solution)/shard_map/all_gather | solution.py:40
  233.7 325.3 %reduce-scatter.2.cloned.1.call-start = ((), (), s32[]{:S(2)}) async-start(), calls=%async_computation.4 | async-start | bytes 1622016 | tf_op jit(solution)/shard_map/reduce_scatter | solution.py:48
Sparse Core Ops, SparseCore 0:
  10.3 132.2 all-gather.3
  144.6 80.6 all-gather.5
  233.8 175.3 all-gather.7
  416.2 142.7 reduce-scatter.1
where the time goes:
time: 571 us; the launch traced here: 567 us
  waiting for transfers between devices  532 us (93%)
  between operations  13.2 us (2%)
  matrix products  9.44 us (2%)
  local copies, waits for them, and re-layouts  9.26 us (2%)
    all_gather x1, waiting for transfers between devices, local(): lax.all_gather(contracted.astype(jnp.bfloat16), 'col', axis=3, tiled=True)  175 us
    reduce_scatter x1, waiting for transfers between devices, local(): lax.psum_scatter(partial_grad, 'row', scatter_dimension=2, tiled=True)  143 us
    all_gather x1, waiting for transfers between devices, local(): whole_site = lax.all_gather(site_tensor, 'col', axis=2, tiled=True)  132 us
    all_gather x1, waiting for transfers between devices, project(): gathered = lax.all_gather(env_panel, 'row', axis=0, tiled=True)  80 us
  transfers between devices with their start and end apart: 4, of which 4 were waited for; matrix products, arithmetic and copies ran while one was open for 1% of the time, Pallas kernels for 0%

commit v1 on v0

v1 whole, which is shorter than its diff:
```python
import jax
import jax.numpy as jnp
from jax import lax
from jax.experimental import pallas as pl
from jax.experimental.pallas import tpu as pltpu
from jax.sharding import PartitionSpec as P

MESH = pl.DeviceIdType.MESH
BF16 = jnp.bfloat16
F32 = jnp.float32

N_COPIES = 128
NX, NZL, NY, NZH = 4, 4, 4, 4


def kernel(
    site_ref, right_ref, left_ref, out_idx_ref, in_idx_ref, ops_ref, result_ref,
    site_all, right_all, chan_all, mixed, expand, keep, to_sibling, from_sibling, to_x, from_x, to_z, from_z,
    send_sems, recv_sems, x_send, x_recv,
):
    r = lax.axis_index("row")
    c = lax.axis_index("col")
    x, zl, k = r // 8, (r // 2) % 4, r % 2
    y, zh = c // 4, c % 4

    def row_of(dx=0, dz=0, dk=0):
        return ((x + dx + 4) % 4) * 8 + ((zl + dz + 4) % 4) * 2 + (k + dk) % 2

    def col_of(dy=0, dz=0):
        return ((y + dy + 4) % 4) * 4 + (zh + dz + 4) % 4

    sibling = (row_of(dk=1), c)
    z_up, z_down = (r, col_of(dz=1)), (r, col_of(dz=-1))
    y_up, y_down = (r, col_of(dy=1)), (r, col_of(dy=-1))
    x_up, x_down, x_far = (row_of(dx=1), c), (row_of(dx=-1), c), (row_of(dx=2), c)
    line = [(row_of(dz=d), c) for d in (1, 2, 3)]

    barrier = pltpu.get_barrier_semaphore()
    partners = [sibling, z_up, z_down, y_up, y_down, x_up, x_down, x_far] + line
    for partner in partners:
        pl.semaphore_signal(barrier, inc=1, device_id=partner, device_id_type=MESH)
    pl.semaphore_wait(barrier, len(partners))

    started = []

    def send(src, dst, device):
        n = len(started)
        copy = pltpu.make_async_remote_copy(
            src_ref=src, dst_ref=dst, send_sem=send_sems.at[n], recv_sem=recv_sems.at[n],
            device_id=device, device_id_type=MESH,
        )
        copy.start()
        started.append(copy)
        return n

    def arrive(n, dst, device):
        pltpu.make_async_remote_copy(
            src_ref=dst, dst_ref=dst, send_sem=send_sems.at[n], recv_sem=recv_sems.at[n],
            device_id=device, device_id_type=MESH,
        ).wait_recv()

    class Ring:
        def __init__(self, at, up, down, low, high, far):
            self.at, self.up, self.down = at, up, down
            self.low, self.high, self.far = low, high, far

        def begin(self, src, own):
            self.n_up = send(src, self.at(own), self.up)
            self.n_down = send(src, self.at(own), self.down)

        def near(self):
            arrive(self.n_up, self.at(self.low), self.down)
            self.n_low = send(self.at(self.low).at[0], self.at(self.low).at[0], self.up)
            arrive(self.n_down, self.at(self.high), self.up)
            self.n_high = send(self.at(self.high).at[1], self.at(self.high).at[1], self.down)

        def end(self):
            arrive(self.n_low, self.at(self.far).at[0], self.down)
            arrive(self.n_high, self.at(self.far).at[1], self.up)

    right_at = lambda origin: right_all.at[origin]
    rights = []

    def to_core(origin, src=None):
        rights_k.append((send(right_at(origin) if src is None else src, right_at(origin), sibling), origin))

    rights_k = []
    line_n = [send(right_ref, right_at(r), peer) for peer in line]
    site_at = lambda origin: site_all.at[origin]
    site_z = Ring(site_at, z_up, z_down, col_of(dz=-1), col_of(dz=1), col_of(dz=2))
    site_z.begin(site_ref, c)

    def x_ring(dz):
        return Ring(right_at, x_up, x_down, row_of(dx=-1, dz=dz), row_of(dx=1, dz=dz), row_of(dx=2, dz=dz))

    def y_ring(at, dz):
        return Ring(at, y_up, y_down, col_of(dy=-1, dz=dz), col_of(dy=1, dz=dz), col_of(dy=2, dz=dz))

    right_x = {0: x_ring(0)}
    right_x[0].begin(right_ref, r)
    site_y = {0: y_ring(site_at, 0)}
    site_y[0].begin(site_ref, c)
    to_core(r, right_ref)

    site_all[c] = site_ref[...]
    right_all[r] = right_ref[...]

    channel_rows = lax.broadcasted_iota(jnp.int32, (16, 48), 0)
    pick_out = channel_rows == jnp.broadcast_to(out_idx_ref[...], (16, 48))
    pick_in = (channel_rows == jnp.broadcast_to(in_idx_ref[...], (16, 48))).astype(F32).astype(BF16)
    spread = (
        lax.broadcasted_iota(jnp.int32, (128, 16), 0) // 8 == lax.broadcasted_iota(jnp.int32, (128, 16), 1)
    ).astype(F32).astype(BF16)
    same = (lax.broadcasted_iota(jnp.int32, (128, 128), 0) % 8) == (lax.broadcasted_iota(jnp.int32, (128, 128), 1) % 8)
    for s in range(2):
        for t in range(2):
            op = ops_ref[pl.ds(2 * s + t, 1), :].astype(F32)
            picked = jnp.where(pick_out, jnp.broadcast_to(op, (16, 48)), 0.0).astype(BF16)
            dense = lax.dot_general(picked, pick_in, (((1,), (1,)), ((), ())), preferred_element_type=F32).astype(BF16)
            tall = jnp.dot(spread, dense, preferred_element_type=F32).astype(BF16)
            wide = lax.dot_general(tall, spread, (((1,), (1,)), ((), ())), preferred_element_type=F32)
            expand[pl.ds(128 * s, 128), pl.ds(128 * t, 128)] = jnp.where(same, wide, 0.0).astype(BF16)

    def x_near(dz):
        right_x[dz].near()
        to_core(right_x[dz].low)
        to_core(right_x[dz].high)

    def x_end(dz):
        right_x[dz].end()
        to_core(right_x[dz].far)

    def line_arrives(d):
        origin = row_of(dz=-d)
        arrive(line_n[d - 1], right_at(origin), line[4 - d - 1])
        right_x[-d] = x_ring(-d)
        right_x[-d].begin(right_at(origin), origin)
        to_core(origin)

    def site_pass(dz):
        site_y[dz] = y_ring(site_at, dz)
        site_y[dz].begin(site_at(col_of(dz=dz)), col_of(dz=dz))

    x_near(0)
    site_y[0].near()
    line_arrives(1)
    line_arrives(3)
    site_z.near()
    site_pass(-1)
    site_pass(1)
    x_end(0)
    site_y[0].end()
    line_arrives(2)
    x_near(-1)
    x_near(-3)
    site_z.end()
    site_pass(2)
    site_y[-1].near()
    site_y[1].near()
    x_end(-1)
    x_end(-3)
    x_near(-2)
    site_y[-1].end()
    site_y[1].end()
    site_y[2].near()
    x_end(-2)
    site_y[2].end()
    for n, origin in rights_k:
        other = origin + 1 - 2 * k
        arrive(n, right_at(other), sibling)

    mixed[...] = jnp.zeros_like(mixed)

    def add_block(block, carry):
        env = jnp.concatenate(
            [right_all[2 * block].reshape(768, 128), right_all[2 * block + 1].reshape(768, 128)], axis=1
        )
        site = site_all[block].reshape(256, 256)
        update = lax.dot_general(env, site, (((1,), (1,)), ((), ())), preferred_element_type=F32)
        mixed[...] += update.reshape(16, 48, 256)
        return carry

    lax.fori_loop(0, 16, add_block, 0)

    def make_channel(half):
        results = []
        for part in range(3):
            run = mixed[:, pl.ds(pl.multiple_of(half * 24 + part * 8, 8), 8), :].reshape(128, 256).astype(BF16)
            stacked = jnp.concatenate([run[:, :128], run[:, 128:]], axis=0)
            results.append(jnp.dot(expand[...], stacked, preferred_element_type=F32))

        def eight(u, h):
            s, part = u // 3, u % 3
            pieces = [results[part][s * 128 + w * 8:s * 128 + w * 8 + 8, :] for w in range(8 * h, 8 * h + 8)]
            return jnp.concatenate(pieces, axis=1)

        for h in range(2):
            for m in range(3):
                rows = jnp.concatenate([eight(2 * m, h), eight(2 * m + 1, h)], axis=0)
                chan_all[c, half, h, pl.ds(16 * m, 16), :] = rows.astype(BF16)

    halves = [1 - k, k]
    chan_at = [lambda origin: chan_all.at[origin, halves[0]], lambda origin: chan_all.at[origin, halves[1]]]
    chan_z, chan_y = [], [{}, {}]

    def chan_pass(i, dz):
        chan_y[i][dz] = y_ring(chan_at[i], dz)
        chan_y[i][dz].begin(chan_at[i](col_of(dz=dz)), col_of(dz=dz))

    for i in range(2):
        make_channel(halves[i])
        ring = Ring(chan_at[i], z_up, z_down, col_of(dz=-1), col_of(dz=1), col_of(dz=2))
        ring.begin(chan_at[i](c), c)
        chan_z.append(ring)
        chan_pass(i, 0)

    def gradient(dy, i):
        group = (y + dy) % 4
        total = None
        for h in range(2):
            lhs = jnp.concatenate([chan_all[group * 4 + j, halves[i], h] for j in range(4)], axis=0)
            term = jnp.dot(lhs, left_ref[pl.ds(1024 * h, 1024), :], preferred_element_type=F32)
            total = term if total is None else total + term
        return total

    sib_n = {}

    def share_other(dy):
        to_sibling[dy] = gradient(dy, 0).astype(BF16)
        sib_n[dy] = send(to_sibling.at[dy], from_sibling.at[dy], sibling)

    def share_own(dy):
        total = gradient(dy, 1)
        arrive(sib_n[dy], from_sibling.at[dy], sibling)
        total = total + from_sibling[dy].astype(F32)
        group = (y + dy) % 4

        @pl.when(group == x)
        def _():
            keep[...] = total

        @pl.when(group != x)
        def _():
            to_x[dy] = total.astype(BF16)
            pltpu.make_async_remote_copy(
                src_ref=to_x.at[dy], dst_ref=from_x.at[x], send_sem=x_send.at[dy], recv_sem=x_recv.at[x],
                device_id=(group * 8 + zl * 2 + k, c), device_id_type=MESH,
            ).start()

    chan_y[0][0].near()
    chan_y[1][0].near()
    chan_y[0][0].end()
    chan_z[0].near()
    chan_pass(0, -1)
    chan_pass(0, 1)
    chan_y[1][0].end()
    chan_z[1].near()
    chan_pass(1, -1)
    chan_pass(1, 1)
    chan_z[0].end()
    chan_pass(0, 2)
    chan_y[0][-1].near()
    chan_y[0][1].near()
    share_other(0)
    chan_z[1].end()
    chan_pass(1, 2)
    chan_y[1][-1].near()
    chan_y[1][1].near()
    share_own(0)
    chan_y[0][-1].end()
    chan_y[0][1].end()
    chan_y[0][2].near()
    share_other(1)
    share_other(3)
    chan_y[1][-1].end()
    chan_y[1][1].end()
    chan_y[1][2].near()
    share_own(1)
    share_own(3)
    chan_y[0][2].end()
    share_other(2)
    chan_y[1][2].end()
    share_own(2)

    total = keep[...]
    for d in (1, 3, 2):
        origin = (x + d) % 4
        pltpu.make_async_remote_copy(
            src_ref=from_x.at[origin], dst_ref=from_x.at[origin], send_sem=x_send.at[0], recv_sem=x_recv.at[origin],
            device_id=(row_of(dx=d), c), device_id_type=MESH,
        ).wait_recv()
        total = total + from_x[origin].astype(F32)
    keep[...] = total
    for j in range(4):
        to_z[j] = total[j * 48:(j + 1) * 48, :].astype(BF16)
    z_n = [send(to_z.at[(zl + d) % 4], from_z.at[zl], line[d - 1]) for d in (1, 2, 3)]
    final = keep[pl.ds(pl.multiple_of(zl * 48, 48), 48), :]
    for d in (1, 2, 3):
        origin = (zl - d + 4) % 4
        arrive(z_n[d - 1], from_z.at[origin], line[4 - d - 1])
        final = final + from_z[origin].astype(F32)
    result_ref[...] = final.reshape(2, 24, 256).astype(BF16)

    for copy in started:
        copy.wait_send()
    for dy in range(4):
        group = (y + dy) % 4

        @pl.when(group != x)
        def _():
            pltpu.make_async_remote_copy(
                src_ref=to_x.at[dy], dst_ref=from_x.at[x], send_sem=x_send.at[dy], recv_sem=x_recv.at[x],
                device_id=(group * 8 + zl * 2 + k, c), device_id_type=MESH,
            ).wait_send()


def local(site_tensor, left_env, right_env, mpo_out, mpo_in, mpo_ops):
    site = jnp.transpose(site_tensor, (1, 0, 2))
    right = jnp.transpose(right_env, (1, 2, 0)).reshape(2, 384, 128)
    left = left_env.reshape(2048, 256)
    ops = jnp.transpose(mpo_ops, (1, 2, 0)).reshape(4, 48)
    vmem = pl.BlockSpec(memory_space=pltpu.VMEM)
    result = pl.pallas_call(
        kernel,
        out_shape=jax.ShapeDtypeStruct((2, 24, 256), BF16),
        in_specs=[vmem] * 6,
        out_specs=vmem,
        scratch_shapes=[
            pltpu.VMEM((16, 2, 128, 256), BF16),
            pltpu.VMEM((32, 2, 384, 128), BF16),
            pltpu.VMEM((16, 2, 2, 48, 1024), BF16),
            pltpu.VMEM((16, 48, 256), F32),
            pltpu.VMEM((256, 256), BF16),
            pltpu.VMEM((192, 256), F32),
            pltpu.VMEM((4, 192, 256), BF16),
            pltpu.VMEM((4, 192, 256), BF16),
            pltpu.VMEM((4, 192, 256), BF16),
            pltpu.VMEM((4, 192, 256), BF16),
            pltpu.VMEM((4, 48, 256), BF16),
            pltpu.VMEM((4, 48, 256), BF16),
            pltpu.SemaphoreType.DMA((N_COPIES,)),
            pltpu.SemaphoreType.DMA((N_COPIES,)),
            pltpu.SemaphoreType.DMA((4,)),
            pltpu.SemaphoreType.DMA((4,)),
        ],
        compiler_params=pltpu.CompilerParams(
            collective_id=0, has_side_effects=True, vmem_limit_bytes=48 * 1024 * 1024
        ),
        cost_estimate=pl.CostEstimate(flops=3_300_000_000, bytes_accessed=2_000_000, transcendentals=0),
        name="gradient_slab",
    )(site, right, left, mpo_out.reshape(1, 48), mpo_in.reshape(1, 48), ops)
    return jnp.transpose(result, (2, 0, 1))


def solution(mesh):
    return jax.shard_map(
        local,
        mesh=mesh,
        in_specs=(
            P("row", None, "col"),
            P(None, "row", "col"),
            P("row", None, "col"),
            P(),
            P(),
            P(),
        ),
        out_specs=P("col", None, "row"),
        check_vma=False,
    )
```

time: 571 us -> 161 us (0.28)
  the two profiles are of different devices: /device:TPU:1 before, /device:TPU:16 now
where the time goes in v1:
time: 161 us
  Pallas kernels  157 us (98%)
  local copies, waits for them, and re-layouts  3.45 us (2%)
    pallas_call x1, Pallas kernels, local(): pl.pallas_call(kernel, out_shape=jax.ShapeDtypeStruct((2, 24, 256), BF16)...  157 us
    unnamed x12, local copies, waits for them, and re-layouts  3.45 us

profile of v1, /device:TPU:16, one launch (start us, length us, event | category | flops | bytes accessed | tf_op | source)
XLA Modules:
  0.0 160.9 jit_solution(5413618945029139324)
XLA Ops:
  0.0 0.0 copy-start.1
  0.0 0.0 copy-start.4
  0.0 1.0 copy.9
  1.0 0.0 copy-start.2
  1.0 0.0 copy-start.3
  1.0 0.0 copy-done.1
  1.0 0.0 copy-done.4
  1.0 0.6 copy-done.2
  1.7 0.0 copy-done.3
  1.7 0.0 copy-start
  1.7 1.2 copy-done
  2.9 157.4 %gradient_slab.1 = bf16[2,24,256]{2,1,0:T(8,128)(2,1)S(1)} custom-call(bf16[2,128,256]{2,1,0:T(8,128)(2,1)S(1)} %bitcast.13, bf16[2,384,128]{2,1,0:T(8,128)(2,1)S(1)} %bitcast.16, bf16[2048,256]{1,0:T(8,128)(2,1)S(1)} %bitcast.15, s32[1,48]{1,0:T(1,128)S(1)} %bitcast.18, s32[1,48]{1,0:T(1,128)S(1)} %bitcast.19, bf16[4,48]{1,0:T(4,128)(2,1)S(1)} %bitcast.17), custom_call_target="tpu_custom_call" | custom-call | flops 3300000000 | bytes 2000000 | tf_op jit(solution)/shard_map/gradient_slab/pallas_call | solution.py:323
  160.3 0.6 copy.11
Async XLA Ops:
  0.0 1.0 copy-start.1
  0.0 1.0 copy-start.4
  1.0 0.7 copy-start.2
  1.0 0.7 copy-start.3
  1.7 1.2 copy-start

commit v2 on v0

v2 whole, which is shorter than its diff:
```python
import jax
import jax.numpy as jnp
from jax import lax
from jax.experimental import pallas as pl
from jax.experimental.pallas import tpu as pltpu
from jax.sharding import PartitionSpec as P

MESH = pl.DeviceIdType.MESH
BF16 = jnp.bfloat16
F32 = jnp.float32

RUNS = 3
N_COPIES = 144


def kernel(
    site_ref, right_hbm, left_hbm, out_idx_ref, in_idx_ref, ops_ref, result_ref,
    site_all, right_in, right_own, right_line, made_all, chan_all, left, mixed, expand,
    keep_k, keep_y, keep_x, done, to_k, from_k, to_y, from_y, to_x, from_x, to_z, from_z,
    send_sems, recv_sems, local_sems,
):
    r = lax.axis_index("row")
    c = lax.axis_index("col")
    x, zl, k = r // 8, (r // 2) % 4, r % 2
    y, zh = c // 4, c % 4

    def row_of(dx=0, dz=0, dk=0):
        return ((x + dx + 4) % 4) * 8 + ((zl + dz + 4) % 4) * 2 + (k + dk) % 2

    def col_of(dy=0, dz=0):
        return ((y + dy + 4) % 4) * 4 + (zh + dz + 4) % 4

    sibling = (row_of(dk=1), c)
    z_up, z_down = (r, col_of(dz=1)), (r, col_of(dz=-1))
    y_peers = [(r, col_of(dy=d)) for d in (1, 2, 3)]
    x_peers = [(row_of(dx=d), c) for d in (1, 2, 3)]
    line = [(row_of(dz=d), c) for d in (1, 2, 3)]
    y_up, y_down, x_up, x_down = y_peers[0], y_peers[2], x_peers[0], x_peers[2]

    barrier = pltpu.get_barrier_semaphore()
    partners = [sibling, z_up, z_down] + y_peers + x_peers + line
    for partner in partners:
        pl.semaphore_signal(barrier, inc=1, device_id=partner, device_id_type=MESH)

    fetch = pltpu.make_async_copy(right_hbm, right_in, local_sems.at[0])
    fetch.start()
    fetch_left = pltpu.make_async_copy(left_hbm.at[pl.ds(4 * y, 4)], left.at[y], local_sems.at[1])
    fetch_left.start()
    site_all[y, 0] = site_ref[...]
    fetch.wait()
    by_eight = right_in[...].astype(F32).reshape(16, 6, 8, 128)
    for p in range(RUNS):
        run = jnp.concatenate([by_eight[:, p], by_eight[:, 3 + p]], axis=1).astype(BF16)
        right_own[k, x, p] = run
    pl.semaphore_wait(barrier, len(partners))

    started = []

    def send(src, dst, device):
        n = len(started)
        copy = pltpu.make_async_remote_copy(
            src_ref=src, dst_ref=dst, send_sem=send_sems.at[n], recv_sem=recv_sems.at[n],
            device_id=device, device_id_type=MESH,
        )
        copy.start()
        started.append(copy)
        return n

    def arrive(n, dst, device):
        pltpu.make_async_remote_copy(
            src_ref=dst, dst_ref=dst, send_sem=send_sems.at[n], recv_sem=recv_sems.at[n],
            device_id=device, device_id_type=MESH,
        ).wait_recv()

    def to_peers(src, dst, peers, here):
        return [send(src((here + d) % 4), dst(here), peers[d - 1]) for d in (1, 2, 3)]

    def from_peers(copies, dst, peers, here):
        for d in (1, 2, 3):
            arrive(copies[d - 1], dst((here - d + 4) % 4), peers[4 - d - 1])

    def left_at(origin):
        return left.at[origin]

    class Ring:
        def __init__(self, own, low, high, far, up, down, half, places=None):
            self.own, self.low, self.high, self.far, self.up, self.down, self.half = own, low, high, far, up, down, half
            self.places = places or (own, own, half(low, 0), half(high, 1))

        def begin(self):
            self.n_up = send(self.own, self.places[0], self.up)
            self.n_down = send(self.own, self.places[1], self.down)

        def near(self):
            arrive(self.n_up, self.low, self.down)
            self.n_low = send(self.half(self.low, 0), self.places[2], self.up)
            arrive(self.n_down, self.high, self.up)
            self.n_high = send(self.half(self.high, 1), self.places[3], self.down)

        def end(self):
            arrive(self.n_low, self.half(self.far, 0), self.down)
            arrive(self.n_high, self.half(self.far, 1), self.up)

    def first_dim(ref, i):
        return ref.at[i]

    def two_of_four(ref, i):
        return ref.at[pl.ds(2 * i, 2)]

    def half_of_v(ref, i):
        return ref.at[:, pl.ds(8 * i, 8)]

    def x_ring(at):
        return Ring(at(x), at((x + 3) % 4), at((x + 1) % 4), at((x + 2) % 4), x_up, x_down, half_of_v)

    groups = {
        "own": lambda core, origin: right_own.at[core, origin],
        0: lambda core, origin: right_line.at[0, core, origin],
        1: lambda core, origin: right_line.at[1, core, origin],
        2: lambda core, origin: right_line.at[2, core, origin],
    }
    whole = {
        "own": lambda core: right_own.at[core],
        0: lambda core: right_line.at[0, core],
        1: lambda core: right_line.at[1, core],
        2: lambda core: right_line.at[2, core],
    }
    right_x, core_n, line_n = {}, {}, {}

    def x_begin(g):
        right_x[g] = x_ring(lambda origin: groups[g](k, origin))
        right_x[g].begin()

    def x_near(g):
        right_x[g].near()

    def x_end(g):
        right_x[g].end()
        core_n[g] = send(whole[g](k), whole[g](k), sibling)

    def core_end(g):
        arrive(core_n[g], whole[g](1 - k), sibling)

    def line_begin(p):
        line_n[p] = [
            send(right_own.at[k, x, p], right_line.at[p, k, x, d - 1], line[d - 1]) for d in (1, 2, 3)
        ]

    def line_end(p):
        for d in (1, 2, 3):
            arrive(line_n[p][d - 1], right_line.at[p, k, x, d - 1], line[4 - d - 1])

    site_y = {}

    def site_pass(part):
        at = {
            "own": lambda o: site_all.at[o, 0],
            "pair": lambda o: site_all.at[o, pl.ds(1, 2)],
            "far": lambda o: site_all.at[o, 3],
        }[part]
        site_y[part] = Ring(at(y), at((y + 3) % 4), at((y + 1) % 4), at((y + 2) % 4), y_up, y_down, first_dim)
        site_y[part].begin()

    x_begin("own")
    site_here = [site_all.at[y, q] for q in range(4)]
    site_z = Ring(
        site_here[0], site_here[2], site_here[1], site_here[3], z_up, z_down, first_dim,
        (site_here[2], site_here[1], site_here[3].at[0], site_here[3].at[1]),
    )
    site_z.begin()
    site_pass("own")
    left_n = to_peers(lambda to: left_hbm.at[pl.ds(4 * to, 4)], left_at, y_peers, y)

    channel_rows = lax.broadcasted_iota(jnp.int32, (16, 48), 0)
    pick_out = channel_rows == jnp.broadcast_to(out_idx_ref[...], (16, 48))
    pick_in = (channel_rows == jnp.broadcast_to(in_idx_ref[...], (16, 48))).astype(F32).astype(BF16)
    spread = (
        lax.broadcasted_iota(jnp.int32, (128, 16), 0) // 8 == lax.broadcasted_iota(jnp.int32, (128, 16), 1)
    ).astype(F32).astype(BF16)
    same = (lax.broadcasted_iota(jnp.int32, (128, 128), 0) % 8) == (lax.broadcasted_iota(jnp.int32, (128, 128), 1) % 8)
    for s in range(2):
        for t in range(2):
            op = ops_ref[pl.ds(2 * s + t, 1), :].astype(F32)
            picked = jnp.where(pick_out, jnp.broadcast_to(op, (16, 48)), 0.0).astype(BF16)
            dense = lax.dot_general(picked, pick_in, (((1,), (1,)), ((), ())), preferred_element_type=F32).astype(BF16)
            tall = jnp.dot(spread, dense, preferred_element_type=F32).astype(BF16)
            wide = lax.dot_general(tall, spread, (((1,), (1,)), ((), ())), preferred_element_type=F32)
            expand[pl.ds(128 * s, 128), pl.ds(128 * t, 128)] = jnp.where(same, wide, 0.0).astype(BF16)

    def make_channel(p):
        def right_block(core, g, d):
            block = right_own[core, g, p] if d == 0 else right_line[p, core, g, d - 1]
            return block.reshape(256, 128)

        mixed[...] = jnp.zeros_like(mixed)

        def add_blocks(g, carry):
            update = None
            for d in range(4):
                env = jnp.concatenate([right_block(0, g, d), right_block(1, g, d)], axis=1)
                step = (zl - d - zh + 8) % 4
                site = site_all[g, step + (step // 2) * (1 - 2 * (step % 2))].reshape(256, 256)
                term = lax.dot_general(env, site, (((1,), (1,)), ((), ())), preferred_element_type=F32)
                update = term if update is None else update + term
            mixed[...] += update
            return carry

        lax.fori_loop(0, 4, add_blocks, 0)
        by_eight = mixed[...].reshape(16, 2, 8, 256)
        stacked = []
        for i in range(2):
            run = by_eight[:, i].reshape(128, 256).astype(BF16)
            stacked.append(jnp.concatenate([run[:, :128], run[:, 128:]], axis=0))
        made = jnp.dot(expand[...], jnp.concatenate(stacked, axis=1), preferred_element_type=F32)
        for s in range(2):
            for group in range(4):
                pieces = []
                for w in range(4 * group, 4 * group + 4):
                    rows = made[s * 128 + w * 8:s * 128 + w * 8 + 8, :]
                    pieces.append(jnp.concatenate([rows[:, :128], rows[:, 128:]], axis=0))
                made_all[p, group, s] = jnp.concatenate(pieces, axis=1).astype(BF16)

    made_n = {}

    def spread_begin(p):
        run = pl.ds(2 * p, 2)
        chan_all[run, zh, y] = made_all[p, y]
        made_n[p] = to_peers(lambda to: made_all.at[p, to], lambda o: chan_all.at[run, zh, o], y_peers, y)

    def spread_end(p):
        from_peers(made_n[p], lambda o: chan_all.at[pl.ds(2 * p, 2), zh, o], y_peers, y)

    chan_z = {}

    def chan_begin(e, count):
        def at(origin):
            return chan_all.at[pl.ds(e, count), origin]

        chan_z[e] = Ring(
            at(zh), at((zh + 3) % 4), at((zh + 1) % 4), at((zh + 2) % 4), z_up, z_down,
            lambda ref, i: ref.at[:, pl.ds(2 * i, 2)],
        )
        chan_z[e].begin()

    k_n, y_n, x_n, z_n = {}, {}, {}, {}

    def share_k(e, count):
        part = pl.ds(e, count)
        rows = chan_all[part].reshape(count * 256, 512)
        for j in range(4):
            total = jnp.dot(rows, left[j].reshape(512, 256), preferred_element_type=F32)
            total = total.reshape(count * 16, 2, 8, 256)
            first, second = total[:, 0].reshape(count, 128, 256), total[:, 1].reshape(count, 128, 256)
            keep_k[j, part] = jnp.where(k == 0, first, second)
            to_k[part, j] = jnp.where(k == 0, second, first).astype(BF16)
        k_n[e] = send(to_k.at[part], from_k.at[part], sibling)

    def share_y(e, count):
        part = pl.ds(e, count)
        arrive(k_n[e], from_k.at[part], sibling)
        for d in (1, 3, 2):
            to = (y + d) % 4
            to_y[to, part] = (keep_k[to, part] + from_k[part, to].astype(F32)).astype(BF16)
        y_n[e] = to_peers(lambda to: to_y.at[to, part], lambda o: from_y.at[o, part], y_peers, y)
        keep_y[part] = keep_k[y, part] + from_k[part, y].astype(F32)

    def share_x(e, count):
        part = pl.ds(e, count)
        from_peers(y_n[e], lambda o: from_y.at[o, part], y_peers, y)
        total = keep_y[part]
        for d in (1, 3, 2):
            total = total + from_y[(y + d) % 4, part].astype(F32)
        total = total.reshape(count * 4, 4, 8, 256)
        for j in range(4):
            block = total[:, j].reshape(count, 32, 256)
            keep_x[j, part] = block
            to_x[j, part] = block.astype(BF16)
        x_n[e] = to_peers(lambda to: to_x.at[to, part], lambda o: from_x.at[o, part], x_peers, x)

    def share_z(e, count):
        part = pl.ds(e, count)
        from_peers(x_n[e], lambda o: from_x.at[o, part], x_peers, x)
        total = keep_x[x, part]
        for d in (1, 3, 2):
            total = total + from_x[(x + d) % 4, part].astype(F32)
        total = total.reshape(count, 4, 8, 256)
        for j in range(4):
            to_z[j, part] = total[:, j]
        z_n[e] = to_peers(lambda to: to_z.at[to, part], lambda o: from_z.at[o, part], line, zl)

    def share_end(e, count):
        part = pl.ds(e, count)
        from_peers(z_n[e], lambda o: from_z.at[o, part], line, zl)
        total = to_z[zl, part]
        for d in (1, 3, 2):
            total = total + from_z[(zl + d) % 4, part]
        done[part] = total

    def drain(upto):
        while drained[0] < upto:
            started[drained[0]].wait_send()
            drained[0] += 1

    drained = [0]
    x_near("own")
    site_y["own"].near()
    line_begin(0)
    x_end("own")
    site_y["own"].end()
    site_z.near()
    site_pass("pair")
    line_end(0)
    x_begin(0)
    site_y["pair"].near()
    site_z.end()
    site_pass("far")
    line_begin(1)
    x_near(0)
    site_y["pair"].end()
    x_end(0)
    site_y["far"].near()
    core_end("own")
    line_end(1)
    x_begin(1)
    line_begin(2)
    site_y["far"].end()
    core_end(0)

    make_channel(0)
    spread_begin(0)
    x_near(1)
    spread_end(0)
    chan_begin(0, 1)
    chan_begin(1, 1)
    x_end(1)
    line_end(2)
    x_begin(2)
    core_end(1)
    make_channel(1)
    spread_begin(1)
    spread_end(1)
    chan_begin(2, 1)
    chan_begin(3, 1)
    x_near(2)
    chan_z[0].near()
    x_end(2)
    chan_z[1].near()
    core_end(2)
    make_channel(2)
    spread_begin(2)
    chan_z[0].end()
    spread_end(2)
    chan_begin(4, 1)
    chan_begin(5, 1)
    chan_z[2].near()
    chan_z[1].end()
    fetch_left.wait()
    from_peers(left_n, left_at, y_peers, y)
    share_k(0, 2)
    chan_z[3].near()
    share_y(0, 2)
    drain(len(started) - 24)
    chan_z[2].end()
    share_x(0, 2)
    chan_z[4].near()
    chan_z[3].end()
    share_k(2, 2)
    drain(len(started) - 24)
    chan_z[5].near()
    share_y(2, 2)
    share_z(0, 2)
    chan_z[4].end()
    share_x(2, 2)
    chan_z[5].end()
    share_k(4, 2)
    share_z(2, 2)
    share_y(4, 2)
    share_end(0, 2)
    drain(len(started) - 24)
    share_x(4, 2)
    share_end(2, 2)
    drain(len(started) - 9)
    share_z(4, 2)
    drain(len(started) - 3)
    share_end(4, 2)
    for s in range(2):
        result_ref[s] = jnp.concatenate([done[2 * p + s] for p in range(RUNS)], axis=0).astype(BF16)
    drain(len(started))


def local(site_tensor, left_env, right_env, mpo_out, mpo_in, mpo_ops):
    site = jnp.transpose(site_tensor, (1, 0, 2))
    right = jnp.transpose(right_env, (1, 2, 0))
    ops = jnp.transpose(mpo_ops, (1, 2, 0)).reshape(4, 48)
    vmem = pl.BlockSpec(memory_space=pltpu.VMEM)
    hbm = pl.BlockSpec(memory_space=pl.ANY)
    result = pl.pallas_call(
        kernel,
        out_shape=jax.ShapeDtypeStruct((2, 24, 256), BF16),
        in_specs=[vmem, hbm, hbm, vmem, vmem, vmem],
        out_specs=vmem,
        scratch_shapes=[
            pltpu.VMEM((4, 4, 2, 128, 256), BF16),
            pltpu.VMEM((16, 48, 128), BF16),
            pltpu.VMEM((2, 4, RUNS, 16, 16, 128), BF16),
            pltpu.VMEM((RUNS, 2, 4, 3, 16, 16, 128), BF16),
            pltpu.VMEM((RUNS, 4, 2, 16, 512), BF16),
            pltpu.VMEM((2 * RUNS, 4, 4, 16, 512), BF16),
            pltpu.VMEM((4, 4, 128, 256), BF16),
            pltpu.VMEM((256, 256), F32),
            pltpu.VMEM((256, 256), BF16),
            pltpu.VMEM((4, 2 * RUNS, 128, 256), F32),
            pltpu.VMEM((2 * RUNS, 128, 256), F32),
            pltpu.VMEM((4, 2 * RUNS, 32, 256), F32),
            pltpu.VMEM((2 * RUNS, 8, 256), F32),
            pltpu.VMEM((2 * RUNS, 4, 128, 256), BF16),
            pltpu.VMEM((2 * RUNS, 4, 128, 256), BF16),
            pltpu.VMEM((4, 2 * RUNS, 128, 256), BF16),
            pltpu.VMEM((4, 2 * RUNS, 128, 256), BF16),
            pltpu.VMEM((4, 2 * RUNS, 32, 256), BF16),
            pltpu.VMEM((4, 2 * RUNS, 32, 256), BF16),
            pltpu.VMEM((4, 2 * RUNS, 8, 256), F32),
            pltpu.VMEM((4, 2 * RUNS, 8, 256), F32),
            pltpu.SemaphoreType.DMA((N_COPIES,)),
            pltpu.SemaphoreType.DMA((N_COPIES,)),
            pltpu.SemaphoreType.DMA((2,)),
        ],
        compiler_params=pltpu.CompilerParams(
            collective_id=0, has_side_effects=True, vmem_limit_bytes=62 * 1024 * 1024
        ),
        cost_estimate=pl.CostEstimate(flops=3_300_000_000, bytes_accessed=2_000_000, transcendentals=0),
        name="gradient_slab",
    )(site, right, left_env, mpo_out.reshape(1, 48), mpo_in.reshape(1, 48), ops)
    return jnp.transpose(result, (2, 0, 1))


def solution(mesh):
    return jax.shard_map(
        local,
        mesh=mesh,
        in_specs=(
            P("row", None, "col"),
            P(None, "row", "col"),
            P("row", None, "col"),
            P(),
            P(),
            P(),
        ),
        out_specs=P("col", None, "row"),
        check_vma=False,
    )
```

time: 571 us -> 144 us (0.25)
  waiting for transfers between devices: 532 us -> 0 us
  Pallas kernels: 0 us -> 140 us
  between operations: 13.2 us -> 0.01 us
  matrix products: 9.44 us -> 0 us
  local copies, waits for them, and re-layouts: 9.26 us -> 2.9 us
    all_gather x3 -> x0, waiting for transfers between devices: 388 us -> none  [the longest x1 175 us: local(): lax.all_gather(contracted.astype(jnp.bfloat16), 'col', axis=3, tiled=True)]
    reduce_scatter x1 -> x0, waiting for transfers between devices: 143 us -> none  [local(): lax.psum_scatter(partial_grad, 'row', scatter_dimension=2, tiled=True)]
    pallas_call x0 -> x1, Pallas kernels: none -> 140 us  [local(): pl.pallas_call(kernel, out_shape=jax.ShapeDtypeStruct((2, 24, 256), BF16)...]
    dot_general x4 -> x0, matrix products: 9.44 us -> none  [the longest x1 4.61 us: project(): product = jnp.dot(site_rows, gathered, preferred_element_type=jnp.float32)]
  transfers between devices with their start and end apart: 4 -> 0, of which waited for: 4 -> 0; matrix products, arithmetic and copies ran while one was open for 1% -> 0% of each run, Pallas kernels for 0% -> 0%
where the time goes in v2:
time: 144 us; the launch traced here: 143 us
  Pallas kernels  140 us (97%)
  local copies, waits for them, and re-layouts  2.9 us (2%)
    pallas_call x1, Pallas kernels, local(): pl.pallas_call(kernel, out_shape=jax.ShapeDtypeStruct((2, 24, 256), BF16)...  140 us
    unnamed x2, local copies, waits for them, and re-layouts  2.9 us

profile of v2, /device:TPU:1, one launch (start us, length us, event | category | flops | bytes accessed | tf_op | source)
XLA Modules:
  0.0 142.9 jit_solution(7393555390127442394)
XLA Ops:
  0.0 1.6 %copy.9 = bf16[128,2,256]{2,0,1:T(8,128)(2,1)} copy(bf16[128,2,256]{2,1,0:T(2,128)(2,1)} %param.6) | data formatting | bytes 262144 | tf_op args[0]
  1.6 140.0 %gradient_slab.1 = bf16[2,24,256]{2,1,0:T(8,128)(2,1)} custom-call(bf16[2,128,256]{2,1,0:T(8,128)(2,1)} %bitcast.10, bf16[16,48,128]{2,1,0:T(8,128)(2,1)} %bitcast.12, bf16[16,128,256]{2,1,0:T(8,128)(2,1)} %left_hbm.1, s32[1,48]{1,0:T(1,128)} %bitcast.14, s32[1,48]{1,0:T(1,128)} %bitcast.15, bf16[4,48]{1,0:T(4,128)(2,1)} %bitcast.13), custom_call_target="tpu_custom_call" | custom-call | flops 3300000000 | bytes 2000000 | tf_op jit(solution)/shard_map/gradient_slab/pallas_call | solution.py:397
  141.6 1.3 copy.11

commit v3 on v2

--- a/solution.py
+++ b/solution.py
@@ -16,7 +16,7 @@
 def kernel(
     site_ref, right_hbm, left_hbm, out_idx_ref, in_idx_ref, ops_ref, result_ref,
     site_all, right_in, right_own, right_line, made_all, chan_all, left, mixed, expand,
-    keep_k, keep_y, keep_x, done, to_k, from_k, to_y, from_y, to_x, from_x, to_z, from_z,
+    keep_k, keep_y, keep_x, done, keep_first, to_k, from_k, to_first, from_first, to_y, from_y, to_x, from_x, to_z, from_z,
     send_sems, recv_sems, local_sems,
 ):
     r = lax.axis_index("row")
@@ -46,7 +46,8 @@
     fetch.start()
     fetch_left = pltpu.make_async_copy(left_hbm.at[pl.ds(4 * y, 4)], left.at[y], local_sems.at[1])
     fetch_left.start()
-    site_all[y, 0] = site_ref[...]
+    for t in range(2):
+        site_all[y, 0, t] = site_ref[:, t, :]
     fetch.wait()
     by_eight = right_in[...].astype(F32).reshape(16, 6, 8, 128)
     for p in range(RUNS):
@@ -277,12 +278,35 @@
             to_x[j, part] = block.astype(BF16)
         x_n[e] = to_peers(lambda to: to_x.at[to, part], lambda o: from_x.at[o, part], x_peers, x)
 
-    def share_z(e, count):
-        part = pl.ds(e, count)
-        from_peers(x_n[e], lambda o: from_x.at[o, part], x_peers, x)
-        total = keep_x[x, part]
+    def share_x_first(e, count):
+        part = pl.ds(e, count)
+        arrive(k_n[e], from_k.at[part], sibling)
+        for j in range(4):
+            total = (keep_k[j, part] + from_k[part, j].astype(F32)).reshape(count * 4, 4, 8, 256)
+            for to in range(4):
+                block = total[:, to].reshape(count, 32, 256)
+                keep_first[to, part, j] = block
+                to_first[to, part, j] = block.astype(BF16)
+        x_n[e] = to_peers(lambda to: to_first.at[to, part], lambda o: from_first.at[o, part], x_peers, x)
+
+    def share_y_second(e, count):
+        part = pl.ds(e, count)
+        from_peers(x_n[e], lambda o: from_first.at[o, part], x_peers, x)
+        for j in range(4):
+            total = keep_first[x, part, j]
+            for d in (1, 3, 2):
+                total = total + from_first[(x + d) % 4, part, j].astype(F32)
+            keep_x[j, part] = total
+            to_x[j, part] = total.astype(BF16)
+        y_n[e] = to_peers(lambda to: to_x.at[to, part], lambda o: from_x.at[o, part], y_peers, y)
+
+    def share_z(e, count, x_first=False):
+        part = pl.ds(e, count)
+        here = y if x_first else x
+        from_peers((y_n if x_first else x_n)[e], lambda o: from_x.at[o, part], y_peers if x_first else x_peers, here)
+        total = keep_x[here, part]
         for d in (1, 3, 2):
-            total = total + from_x[(x + d) % 4, part].astype(F32)
+            total = total + from_x[(here + d) % 4, part].astype(F32)
         total = total.reshape(count, 4, 8, 256)
         for j in range(4):
             to_z[j, part] = total[:, j]
@@ -306,9 +330,9 @@
     site_y["own"].near()
     line_begin(0)
     x_end("own")
-    site_y["own"].end()
     site_z.near()
     site_pass("pair")
+    site_y["own"].end()
     line_end(0)
     x_begin(0)
     site_y["pair"].near()
@@ -348,48 +372,51 @@
     core_end(2)
     make_channel(2)
     spread_begin(2)
-    chan_z[0].end()
     spread_end(2)
     chan_begin(4, 1)
     chan_begin(5, 1)
+    drain(len(started) - 24)
     chan_z[2].near()
+    chan_z[3].near()
+    chan_z[0].end()
     chan_z[1].end()
     fetch_left.wait()
     from_peers(left_n, left_at, y_peers, y)
     share_k(0, 2)
-    chan_z[3].near()
+    drain(len(started) - 16)
     share_y(0, 2)
-    drain(len(started) - 24)
+    chan_z[4].near()
+    chan_z[5].near()
     chan_z[2].end()
-    share_x(0, 2)
-    chan_z[4].near()
     chan_z[3].end()
     share_k(2, 2)
-    drain(len(started) - 24)
-    chan_z[5].near()
-    share_y(2, 2)
+    share_x(0, 2)
+    share_x_first(2, 2)
+    chan_z[4].end()
+    share_k(4, 1)
+    share_y(4, 1)
+    chan_z[5].end()
+    share_k(5, 1)
     share_z(0, 2)
-    chan_z[4].end()
-    share_x(2, 2)
-    chan_z[5].end()
-    share_k(4, 2)
-    share_z(2, 2)
-    share_y(4, 2)
+    share_x_first(5, 1)
+    share_y_second(2, 2)
+    share_x(4, 1)
+    share_y_second(5, 1)
+    share_z(2, 2, True)
+    share_z(4, 1)
+    share_z(5, 1, True)
     share_end(0, 2)
-    drain(len(started) - 24)
-    share_x(4, 2)
+    drain(len(started) - 16)
     share_end(2, 2)
-    drain(len(started) - 9)
-    share_z(4, 2)
+    share_end(4, 1)
     drain(len(started) - 3)
-    share_end(4, 2)
+    share_end(5, 1)
     for s in range(2):
         result_ref[s] = jnp.concatenate([done[2 * p + s] for p in range(RUNS)], axis=0).astype(BF16)
     drain(len(started))
 
 
 def local(site_tensor, left_env, right_env, mpo_out, mpo_in, mpo_ops):
-    site = jnp.transpose(site_tensor, (1, 0, 2))
     right = jnp.transpose(right_env, (1, 2, 0))
     ops = jnp.transpose(mpo_ops, (1, 2, 0)).reshape(4, 48)
     vmem = pl.BlockSpec(memory_space=pltpu.VMEM)
@@ -413,8 +440,11 @@
             pltpu.VMEM((2 * RUNS, 128, 256), F32),
             pltpu.VMEM((4, 2 * RUNS, 32, 256), F32),
             pltpu.VMEM((2 * RUNS, 8, 256), F32),
+            pltpu.VMEM((4, 2 * RUNS, 4, 32, 256), F32),
             pltpu.VMEM((2 * RUNS, 4, 128, 256), BF16),
             pltpu.VMEM((2 * RUNS, 4, 128, 256), BF16),
+            pltpu.VMEM((4, 2 * RUNS, 4, 32, 256), BF16),
+            pltpu.VMEM((4, 2 * RUNS, 4, 32, 256), BF16),
             pltpu.VMEM((4, 2 * RUNS, 128, 256), BF16),
             pltpu.VMEM((4, 2 * RUNS, 128, 256), BF16),
             pltpu.VMEM((4, 2 * RUNS, 32, 256), BF16),
@@ -430,7 +460,7 @@
         ),
         cost_estimate=pl.CostEstimate(flops=3_300_000_000, bytes_accessed=2_000_000, transcendentals=0),
         name="gradient_slab",
-    )(site, right, left_env, mpo_out.reshape(1, 48), mpo_in.reshape(1, 48), ops)
+    )(site_tensor, right, left_env, mpo_out.reshape(1, 48), mpo_in.reshape(1, 48), ops)
     return jnp.transpose(result, (2, 0, 1))
 
 

time: 144 us -> 135 us (0.938)
  Pallas kernels: 140 us -> 133 us
  local copies, waits for them, and re-layouts: 2.9 us -> 1.35 us
    pallas_call x1, Pallas kernels: 140 us -> 133 us  [local(): pl.pallas_call(kernel, out_shape=jax.ShapeDtypeStruct((2, 24, 256), BF16)...]
    unnamed x2 -> x1, local copies, waits for them, and re-layouts: 2.9 us -> 1.35 us
where the time goes in v3:
time: 135 us; the launch traced here: 134 us
  Pallas kernels  133 us (99%)
  local copies, waits for them, and re-layouts  1.35 us (1%)
    pallas_call x1, Pallas kernels, local(): pl.pallas_call(kernel, out_shape=jax.ShapeDtypeStruct((2, 24, 256), BF16)...  133 us

profile of v3, /device:TPU:1, one launch (start us, length us, event | category | flops | bytes accessed | tf_op | source)
XLA Modules:
  0.0 134.3 jit_solution(4659315297378286003)
XLA Ops:
  0.0 133.0 %gradient_slab.1 = bf16[2,24,256]{2,1,0:T(8,128)(2,1)} custom-call(bf16[128,2,256]{2,1,0:T(2,128)(2,1)} %site_ref.1, bf16[16,48,128]{2,1,0:T(8,128)(2,1)} %bitcast.8, bf16[16,128,256]{2,1,0:T(8,128)(2,1)} %left_hbm.1, s32[1,48]{1,0:T(1,128)} %bitcast.10, s32[1,48]{1,0:T(1,128)} %bitcast.11, bf16[4,48]{1,0:T(4,128)(2,1)} %bitcast.9), custom_call_target="tpu_custom_call" | custom-call | flops 3300000000 | bytes 2000000 | tf_op jit(solution)/shard_map/gradient_slab/pallas_call | solution.py:424
  133.0 1.3 %copy.8 = bf16[256,2,24]{0,2,1:T(8,128)(2,1)} copy(bf16[256,2,24]{0,2,1:T(8,128)(2,1)} %bitcast.7) | data formatting | bytes 49152

commit v4 on v3

--- a/solution.py
+++ b/solution.py
@@ -15,7 +15,7 @@
 
 def kernel(
     site_ref, right_hbm, left_hbm, out_idx_ref, in_idx_ref, ops_ref, result_ref,
-    site_all, right_in, right_own, right_line, made_all, chan_all, left, mixed, expand,
+    site_all, right_in, right_own, right_line, made_first, made_all, chan_all, left, mixed, expand,
     keep_k, keep_y, keep_x, done, keep_first, to_k, from_k, to_first, from_first, to_y, from_y, to_x, from_x, to_z, from_z,
     send_sems, recv_sems, local_sems,
 ):
@@ -219,7 +219,11 @@
                 for w in range(4 * group, 4 * group + 4):
                     rows = made[s * 128 + w * 8:s * 128 + w * 8 + 8, :]
                     pieces.append(jnp.concatenate([rows[:, :128], rows[:, 128:]], axis=0))
-                made_all[p, group, s] = jnp.concatenate(pieces, axis=1).astype(BF16)
+                rows = jnp.concatenate(pieces, axis=1).astype(BF16)
+                if p == 0:
+                    made_first[zh, group, s] = rows
+                else:
+                    made_all[p, group, s] = rows
 
     made_n = {}
 
@@ -230,6 +234,23 @@
 
     def spread_end(p):
         from_peers(made_n[p], lambda o: chan_all.at[pl.ds(2 * p, 2), zh, o], y_peers, y)
+
+    first = Ring(
+        made_first.at[zh], made_first.at[(zh + 3) % 4], made_first.at[(zh + 1) % 4], made_first.at[(zh + 2) % 4],
+        z_up, z_down, two_of_four,
+    )
+    first_n = {}
+
+    def first_spread(dz):
+        origin = (zh + dz) % 4
+        chan_all[pl.ds(0, 2), origin, y] = made_first[origin, y]
+        first_n[dz] = to_peers(
+            lambda to: made_first.at[origin, to], lambda o: chan_all.at[pl.ds(0, 2), origin, o], y_peers, y
+        )
+
+    def first_spread_end(dz):
+        origin = (zh + dz) % 4
+        from_peers(first_n[dz], lambda o: chan_all.at[pl.ds(0, 2), origin, o], y_peers, y)
 
     chan_z = {}
 
@@ -351,11 +372,9 @@
     core_end(0)
 
     make_channel(0)
-    spread_begin(0)
+    first.begin()
+    first_spread(0)
     x_near(1)
-    spread_end(0)
-    chan_begin(0, 1)
-    chan_begin(1, 1)
     x_end(1)
     line_end(2)
     x_begin(2)
@@ -366,9 +385,10 @@
     chan_begin(2, 1)
     chan_begin(3, 1)
     x_near(2)
-    chan_z[0].near()
+    first.near()
+    first_spread(3)
+    first_spread(1)
     x_end(2)
-    chan_z[1].near()
     core_end(2)
     make_channel(2)
     spread_begin(2)
@@ -377,37 +397,44 @@
     chan_begin(5, 1)
     drain(len(started) - 24)
     chan_z[2].near()
+    first.end()
+    first_spread(2)
     chan_z[3].near()
-    chan_z[0].end()
-    chan_z[1].end()
     fetch_left.wait()
     from_peers(left_n, left_at, y_peers, y)
+    for dz in range(4):
+        first_spread_end(dz)
     share_k(0, 2)
     drain(len(started) - 16)
     share_y(0, 2)
     chan_z[4].near()
     chan_z[5].near()
     chan_z[2].end()
+    share_k(2, 1)
     chan_z[3].end()
-    share_k(2, 2)
+    share_k(3, 1)
     share_x(0, 2)
-    share_x_first(2, 2)
+    share_y(2, 1)
+    share_x_first(3, 1)
     chan_z[4].end()
     share_k(4, 1)
+    share_z(0, 2)
     share_y(4, 1)
     chan_z[5].end()
     share_k(5, 1)
-    share_z(0, 2)
+    share_x(2, 1)
     share_x_first(5, 1)
-    share_y_second(2, 2)
+    share_y_second(3, 1)
     share_x(4, 1)
+    share_z(2, 1)
     share_y_second(5, 1)
-    share_z(2, 2, True)
+    share_z(3, 1, True)
     share_z(4, 1)
+    share_end(0, 2)
+    share_end(2, 1)
     share_z(5, 1, True)
-    share_end(0, 2)
     drain(len(started) - 16)
-    share_end(2, 2)
+    share_end(3, 1)
     share_end(4, 1)
     drain(len(started) - 3)
     share_end(5, 1)
@@ -431,6 +458,7 @@
             pltpu.VMEM((16, 48, 128), BF16),
             pltpu.VMEM((2, 4, RUNS, 16, 16, 128), BF16),
             pltpu.VMEM((RUNS, 2, 4, 3, 16, 16, 128), BF16),
+            pltpu.VMEM((4, 4, 2, 16, 512), BF16),
             pltpu.VMEM((RUNS, 4, 2, 16, 512), BF16),
             pltpu.VMEM((2 * RUNS, 4, 4, 16, 512), BF16),
             pltpu.VMEM((4, 4, 128, 256), BF16),

time: 135 us -> 133 us (0.985)
  Pallas kernels: 133 us -> 131 us
    pallas_call x1, Pallas kernels: 133 us -> 131 us  [local(): pl.pallas_call(kernel, out_shape=jax.ShapeDtypeStruct((2, 24, 256), BF16)...]
where the time goes in v4:
time: 133 us; the launch traced here: 132 us
  Pallas kernels  131 us (98%)
  local copies, waits for them, and re-layouts  1.35 us (1%)
    pallas_call x1, Pallas kernels, local(): pl.pallas_call(kernel, out_shape=jax.ShapeDtypeStruct((2, 24, 256), BF16)...  131 us

profile of v4, /device:TPU:1, one launch (start us, length us, event | category | flops | bytes accessed | tf_op | source)
XLA Modules:
  0.0 132.2 jit_solution(9262309119691699891)
XLA Ops:
  0.0 130.8 %gradient_slab.1 = bf16[2,24,256]{2,1,0:T(8,128)(2,1)} custom-call(bf16[128,2,256]{2,1,0:T(2,128)(2,1)} %site_ref.1, bf16[16,48,128]{2,1,0:T(8,128)(2,1)} %bitcast.8, bf16[16,128,256]{2,1,0:T(8,128)(2,1)} %left_hbm.1, s32[1,48]{1,0:T(1,128)} %bitcast.10, s32[1,48]{1,0:T(1,128)} %bitcast.11, bf16[4,48]{1,0:T(4,128)(2,1)} %bitcast.9), custom_call_target="tpu_custom_call" | custom-call | flops 3300000000 | bytes 2000000 | tf_op jit(solution)/shard_map/gradient_slab/pallas_call | solution.py:451
  130.8 1.3 %copy.8 = bf16[256,2,24]{0,2,1:T(8,128)(2,1)} copy(bf16[256,2,24]{0,2,1:T(8,128)(2,1)} %bitcast.7) | data formatting | bytes 49152

commit v5 on v4

--- a/solution.py
+++ b/solution.py
@@ -162,13 +162,13 @@
         site_y[part] = Ring(at(y), at((y + 3) % 4), at((y + 1) % 4), at((y + 2) % 4), y_up, y_down, first_dim)
         site_y[part].begin()
 
-    x_begin("own")
     site_here = [site_all.at[y, q] for q in range(4)]
     site_z = Ring(
         site_here[0], site_here[2], site_here[1], site_here[3], z_up, z_down, first_dim,
         (site_here[2], site_here[1], site_here[3].at[0], site_here[3].at[1]),
     )
     site_z.begin()
+    x_begin("own")
     site_pass("own")
     left_n = to_peers(lambda to: left_hbm.at[pl.ds(4 * to, 4)], left_at, y_peers, y)
 
@@ -383,9 +383,9 @@
     spread_begin(1)
     spread_end(1)
     chan_begin(2, 1)
-    chan_begin(3, 1)
     x_near(2)
     first.near()
+    chan_begin(3, 1)
     first_spread(3)
     first_spread(1)
     x_end(2)
@@ -394,9 +394,9 @@
     spread_begin(2)
     spread_end(2)
     chan_begin(4, 1)
-    chan_begin(5, 1)
     drain(len(started) - 24)
     chan_z[2].near()
+    chan_begin(5, 1)
     first.end()
     first_spread(2)
     chan_z[3].near()
@@ -418,12 +418,12 @@
     share_x_first(3, 1)
     chan_z[4].end()
     share_k(4, 1)
-    share_z(0, 2)
     share_y(4, 1)
     chan_z[5].end()
     share_k(5, 1)
     share_x(2, 1)
     share_x_first(5, 1)
+    share_z(0, 2)
     share_y_second(3, 1)
     share_x(4, 1)
     share_z(2, 1)

time: 133 us -> 132 us (level)
  Pallas kernels: 131 us -> 129 us
    pallas_call x1, Pallas kernels: 131 us -> 129 us  [local(): pl.pallas_call(kernel, out_shape=jax.ShapeDtypeStruct((2, 24, 256), BF16)...]
where the time goes in v5:
time: 132 us; the launch traced here: 130 us
  Pallas kernels  129 us (98%)
  local copies, waits for them, and re-layouts  1.35 us (1%)
    pallas_call x1, Pallas kernels, local(): pl.pallas_call(kernel, out_shape=jax.ShapeDtypeStruct((2, 24, 256), BF16)...  129 us

profile of v5, /device:TPU:1, one launch (start us, length us, event | category | flops | bytes accessed | tf_op | source)
XLA Modules:
  0.0 130.4 jit_solution(6687577165783675127)
XLA Ops:
  0.0 129.0 %gradient_slab.1 = bf16[2,24,256]{2,1,0:T(8,128)(2,1)} custom-call(bf16[128,2,256]{2,1,0:T(2,128)(2,1)} %site_ref.1, bf16[16,48,128]{2,1,0:T(8,128)(2,1)} %bitcast.8, bf16[16,128,256]{2,1,0:T(8,128)(2,1)} %left_hbm.1, s32[1,48]{1,0:T(1,128)} %bitcast.10, s32[1,48]{1,0:T(1,128)} %bitcast.11, bf16[4,48]{1,0:T(4,128)(2,1)} %bitcast.9), custom_call_target="tpu_custom_call" | custom-call | flops 3300000000 | bytes 2000000 | tf_op jit(solution)/shard_map/gradient_slab/pallas_call | solution.py:451
  129.0 1.3 %copy.8 = bf16[256,2,24]{0,2,1:T(8,128)(2,1)} copy(bf16[256,2,24]{0,2,1:T(8,128)(2,1)} %bitcast.7) | data formatting | bytes 49152

commit v6 on v5

--- a/solution.py
+++ b/solution.py
@@ -396,10 +396,10 @@
     chan_begin(4, 1)
     drain(len(started) - 24)
     chan_z[2].near()
+    chan_z[3].near()
     chan_begin(5, 1)
     first.end()
     first_spread(2)
-    chan_z[3].near()
     fetch_left.wait()
     from_peers(left_n, left_at, y_peers, y)
     for dz in range(4):

time: 132 us -> 133 us (level); the launches traced: 130 us -> 133 us
  Pallas kernels: 129 us -> 131 us
    pallas_call x1, Pallas kernels: 129 us -> 131 us  [local(): pl.pallas_call(kernel, out_shape=jax.ShapeDtypeStruct((2, 24, 256), BF16)...]
where the time goes in v6:
time: 133 us
  Pallas kernels  131 us (98%)
  local copies, waits for them, and re-layouts  1.35 us (1%)
    pallas_call x1, Pallas kernels, local(): pl.pallas_call(kernel, out_shape=jax.ShapeDtypeStruct((2, 24, 256), BF16)...  131 us

profile of v6, /device:TPU:1, one launch (start us, length us, event | category | flops | bytes accessed | tf_op | source)
XLA Modules:
  0.0 132.9 jit_solution(14910356015104854075)
XLA Ops:
  0.0 131.5 %gradient_slab.1 = bf16[2,24,256]{2,1,0:T(8,128)(2,1)} custom-call(bf16[128,2,256]{2,1,0:T(2,128)(2,1)} %site_ref.1, bf16[16,48,128]{2,1,0:T(8,128)(2,1)} %bitcast.8, bf16[16,128,256]{2,1,0:T(8,128)(2,1)} %left_hbm.1, s32[1,48]{1,0:T(1,128)} %bitcast.10, s32[1,48]{1,0:T(1,128)} %bitcast.11, bf16[4,48]{1,0:T(4,128)(2,1)} %bitcast.9), custom_call_target="tpu_custom_call" | custom-call | flops 3300000000 | bytes 2000000 | tf_op jit(solution)/shard_map/gradient_slab/pallas_call | solution.py:451
  131.5 1.3 %copy.8 = bf16[256,2,24]{0,2,1:T(8,128)(2,1)} copy(bf16[256,2,24]{0,2,1:T(8,128)(2,1)} %bitcast.7) | data formatting | bytes 49152
